TPU v7x, 32 devices: a whole 2x2x4 slice. The times are simulated.
32 devices in a mesh: groups: 2 (over y), ctx: 4 (over z), mp: 4 (over x, core).
Axes of the slice: x: 2, y: 2, z: 4, core: 2. Of those that a mesh axis runs over, the one named last changes fastest.
Arguments:
- block_entry_input: bfloat16 [1536, 2048], P('mp', ('groups', 'ctx')), parts along dimension 1, may hold values from -6 to 6
- first_conv_taps: bfloat16 [3, 768, 1536], P(None, 'mp'), may hold values from -0.09375 to 0.09375
- first_pointwise_weight: bfloat16 [1536, 768], P(None, 'mp'), may hold values from -0.21875 to 0.21875
- second_conv_taps: bfloat16 [3, 768, 1536], P(None, 'mp'), may hold values from -0.09375 to 0.09375
- second_pointwise_weight: bfloat16 [1536, 768], P(None, 'mp'), may hold values from -0.21875 to 0.21875
- grad_heads: bfloat16 [8, 192, 2048], P('mp', 'ctx', 'groups'), parts along dimension 2, may hold values from -6 to 6
Outputs:
- second_block_output: bfloat16 [1536, 2048], P('mp', ('groups', 'ctx')), parts along dimension 1
- entry_input_gradient: bfloat16 [1536, 2048], P('mp', ('groups', 'ctx')), parts along dimension 1
- first_taps_gradient: float32 [6, 768, 1536], P('groups', 'mp', 'ctx'), parts along dimension 0
- first_projection_gradient: float32 [3072, 768], P(('groups', 'ctx'), 'mp'), parts along dimension 0
- second_taps_gradient: float32 [6, 768, 1536], P('groups', 'mp', 'ctx'), parts along dimension 0
- second_projection_gradient: float32 [3072, 768], P(('groups', 'ctx'), 'mp'), parts along dimension 0
There are 2 independent parts, one for each index of `groups`. A program takes and returns all parts, laid end to end along the dimension named above; an argument that names none is the same for every part. Nothing has to cross between parts.
All inputs are finite; a program needn't handle non-finite values.
Results may differ from a plain program's by a relative error of at most 0.034.
Values may be sent and summed in bfloat16 or wider, within the bound.
A program may use at most 192 MiB of HBM per device.

v0:
```python
import jax
import jax.numpy as jnp
from jax import lax
from jax.sharding import PartitionSpec as P

FIRST_DILATION = 1024
SECOND_DILATION = 2048


def shifted(value, axis, by):
    length = lax.axis_size(axis)
    pairs = [(i, i + by) for i in range(length) if 0 <= i + by < length]
    return lax.ppermute(value, axis, pairs)


def gelu_slope(values):
    return jax.jvp(jax.nn.gelu, (values,), (jnp.ones_like(values),))[1]


def contract_first(left, right):
    return lax.dot_general(
        left, right, (((0,), (0,)), ((), ())), preferred_element_type=jnp.float32
    )


def contract_last(left, right):
    return lax.dot_general(
        left, right, (((1,), (1,)), ((), ())), preferred_element_type=jnp.float32
    )


def hop_steps(activations, dilation):
    return dilation // activations.shape[1]


def residual_block_forward(activations, conv_weight, point_weight, dilation):
    hop_count = hop_steps(activations, dilation)
    squash_part = jax.nn.gelu(activations.astype(jnp.float32)).astype(jnp.bfloat16)
    squashed = lax.all_gather(squash_part, "mp", axis=0, tiled=True)
    earlier = shifted(squashed, "ctx", hop_count)
    later = shifted(squashed, "ctx", -hop_count)
    pre_act = jnp.dot(conv_weight[0], earlier, preferred_element_type=jnp.float32)
    pre_act = pre_act + jnp.dot(conv_weight[1], squashed, preferred_element_type=jnp.float32)
    pre_act = pre_act + jnp.dot(conv_weight[2], later, preferred_element_type=jnp.float32)
    hidden = jax.nn.gelu(pre_act).astype(jnp.bfloat16)
    mixed = lax.psum_scatter(
        jnp.dot(point_weight, hidden, preferred_element_type=jnp.float32).astype(jnp.bfloat16),
        "mp",
        scatter_dimension=0,
        tiled=True,
    ).astype(jnp.float32)
    result = (activations.astype(jnp.float32) + mixed).astype(jnp.bfloat16)
    return (result, squashed, pre_act, hidden)


def residual_block_backward(
    incoming_gradient, activations, squashed, pre_act, hidden, conv_weight, point_weight, dilation
):
    hop_count = hop_steps(activations, dilation)
    upstream_full = lax.all_gather(incoming_gradient, "mp", axis=0, tiled=True)
    grad_hidden = contract_first(point_weight, upstream_full)
    grad_pre = (grad_hidden * gelu_slope(pre_act)).astype(jnp.bfloat16)
    grad_later = shifted(grad_pre, "ctx", -hop_count)
    grad_earlier = shifted(grad_pre, "ctx", hop_count)
    moved = (grad_later, grad_pre, grad_earlier)
    grad_conv = jnp.stack(
        [
            contract_last(moved[0], squashed),
            contract_last(moved[1], squashed),
            contract_last(moved[2], squashed),
        ]
    )
    grad_point = contract_last(upstream_full, hidden)
    total = contract_first(conv_weight[0], moved[0])
    total = total + contract_first(conv_weight[1], moved[1])
    grad_squash = lax.psum_scatter(
        (total + contract_first(conv_weight[2], moved[2])).astype(jnp.bfloat16),
        "mp",
        scatter_dimension=0,
        tiled=True,
    ).astype(jnp.float32)
    previous = (
        incoming_gradient.astype(jnp.float32)
        + grad_squash * gelu_slope(activations.astype(jnp.float32))
    ).astype(jnp.bfloat16)
    return (previous, grad_conv, grad_point)


def reduce_block(grad_conv, grad_point):
    return (
        lax.psum_scatter(
            grad_conv.astype(jnp.bfloat16), "ctx", scatter_dimension=2, tiled=True
        ).astype(jnp.float32),
        lax.psum_scatter(
            grad_point.astype(jnp.bfloat16), "ctx", scatter_dimension=0, tiled=True
        ).astype(jnp.float32),
    )


def shards(
    block_entry_input,
    first_conv_taps,
    first_pointwise_weight,
    second_conv_taps,
    second_pointwise_weight,
    grad_heads,
):
    regrouped = lax.all_to_all(grad_heads, "ctx", split_axis=2, concat_axis=1, tiled=True)
    incoming_gradient = regrouped.reshape(
        regrouped.shape[0] * regrouped.shape[1], regrouped.shape[2]
    )
    between_blocks_state, first_gelu_output, first_preactivation, first_hidden_state = (
        residual_block_forward(
            block_entry_input, first_conv_taps, first_pointwise_weight, FIRST_DILATION
        )
    )
    second_block_output, second_gelu_output, second_preactivation, second_hidden_state = (
        residual_block_forward(
            between_blocks_state, second_conv_taps, second_pointwise_weight, SECOND_DILATION
        )
    )
    incoming_gradient, conv_grad_b, point_grad_b = residual_block_backward(
        incoming_gradient,
        between_blocks_state,
        second_gelu_output,
        second_preactivation,
        second_hidden_state,
        second_conv_taps,
        second_pointwise_weight,
        SECOND_DILATION,
    )
    conv_grad_b, point_grad_b = reduce_block(conv_grad_b, point_grad_b)
    entry_input_gradient, conv_grad_a, point_grad_a = residual_block_backward(
        incoming_gradient,
        block_entry_input,
        first_gelu_output,
        first_preactivation,
        first_hidden_state,
        first_conv_taps,
        first_pointwise_weight,
        FIRST_DILATION,
    )
    conv_grad_a, point_grad_a = reduce_block(conv_grad_a, point_grad_a)
    return (
        second_block_output,
        entry_input_gradient,
        conv_grad_a,
        point_grad_a,
        conv_grad_b,
        point_grad_b,
    )


def solution(mesh):
    placed = (
        P("mp", ("groups", "ctx")),
        P(None, "mp", None),
        P(None, "mp"),
        P(None, "mp", None),
        P(None, "mp"),
        P("mp", "ctx", "groups"),
    )
    return jax.shard_map(
        shards,
        mesh=mesh,
        in_specs=placed,
        out_specs=(
            P("mp", ("groups", "ctx")),
            P("mp", ("groups", "ctx")),
            P("groups", "mp", "ctx"),
            P(("groups", "ctx"), "mp"),
            P("groups", "mp", "ctx"),
            P(("groups", "ctx"), "mp"),
        ),
        check_vma=False,
    )
```

profile of v0, /device:TPU:0, one launch (start us, length us, event | category | flops | bytes accessed | tf_op | source)
XLA Modules:
  0.0 296.0 jit_solution(17952154528425579025)
XLA Ops:
  7.2 1.2 fusion.62
  8.5 10.0 %all_gather.12 = bf16[1536,256]{1,0:T(8,128)(2,1)S(1)} all-gather(bf16[384,256]{1,0:T(8,128)(2,1)S(1)} %fusion.62), channel_id=1, replica_groups=mesh['groups'=2,'ctx'=4,'mp'=4] {'mp'}, dimensions={0}, use_global_device_ids=true | all-gather | bytes 983040 | tf_op jit(solution)/shard_map/all_gather | solution.py:39
  19.2 1.4 fusion.33
  22.1 1.2 copy.33
  23.3 24.3 %reduce-scatter.25.cloned.1.call-done = bf16[384,256]{1,0:T(8,128)(2,1)} async-done(((bf16[1536,256]{1,0:T(8,128)(2,1)}), bf16[384,256]{1,0:T(8,128)(2,1)}) %reduce-scatter.25.cloned.1.call-update) | async-done | bytes 196624 | tf_op jit(solution)/shard_map/reduce_scatter | solution.py:46
  47.6 1.1 fusion.71
  48.7 8.2 %all_gather.13 = bf16[1536,256]{1,0:T(8,128)(2,1)S(1)} all-gather(bf16[384,256]{1,0:T(8,128)(2,1)S(1)} %fusion.71), channel_id=1, replica_groups=mesh['groups'=2,'ctx'=4,'mp'=4] {'mp'}, dimensions={0}, use_global_device_ids=true | all-gather | bytes 983040 | tf_op jit(solution)/shard_map/all_gather | solution.py:39
  56.9 1.5 collective-permute-start.1
  58.8 1.5 reshape.35
  60.3 4.6 %all-to-all-start = ((bf16[4,2,12288]{2,1,0:T(2,128)(2,1)}), bf16[4,2,12288]{2,1,0:T(2,128)(2,1)}, u32[]{:S(2)}, u32[]{:S(2)}) async-start(bf16[4,2,12288]{2,1,0:T(2,128)(2,1)} %reshape.35), calls=%async_computation | async-start | bytes 393216 | tf_op jit(solution)/shard_map/all_to_all | solution.py:108
  64.9 1.4 fusion.23
  66.3 1.6 fusion.19
  68.0 1.6 fusion.16
  70.1 1.2 copy.35
  71.3 1.7 all-to-all-done
  73.0 1.4 reshape.36
  75.6 8.0 %all_gather.14 = bf16[1536,256]{1,0:T(8,128)(2,1)S(1)} all-gather(bf16[384,256]{1,0:T(8,128)(2,1)S(1)} %bitcast.104), channel_id=1, replica_groups=mesh['groups'=2,'ctx'=4,'mp'=4] {'mp'}, dimensions={0}, use_global_device_ids=true | all-gather | bytes 983040 | tf_op jit(solution)/shard_map/all_gather | solution.py:60
  86.1 1.2 copy.37
  87.3 1.7 fusion.12
  89.0 1.2 copy.47
  90.2 5.3 %reduce-scatter.27.cloned.1.call-done = bf16[384,256]{1,0:T(8,128)(2,1)} async-done(((bf16[1536,256]{1,0:T(8,128)(2,1)}), bf16[384,256]{1,0:T(8,128)(2,1)}) %reduce-scatter.27.cloned.1.call-update) | async-done | bytes 196624 | tf_op jit(solution)/shard_map/reduce_scatter | solution.py:46
  95.5 26.4 %reduce-scatter.29.cloned.1.call-done = bf16[384,256]{1,0:T(8,128)(2,1)} async-done(((bf16[1536,256]{1,0:T(8,128)(2,1)}), bf16[384,256]{1,0:T(8,128)(2,1)}) %reduce-scatter.29.cloned.1.call-update) | async-done | bytes 196624 | tf_op jit(solution)/shard_map/reduce_scatter | solution.py:76
  121.9 2.1 fusion.76
  124.1 8.2 %all_gather.15 = bf16[1536,256]{1,0:T(8,128)(2,1)S(1)} all-gather(bf16[384,256]{1,0:T(8,128)(2,1)S(1)} %get-tuple-element.24), channel_id=1, replica_groups=mesh['groups'=2,'ctx'=4,'mp'=4] {'mp'}, dimensions={0}, use_global_device_ids=true | all-gather | bytes 983040 | tf_op jit(solution)/shard_map/all_gather | solution.py:60
  132.3 1.2 convolution_convert_fusion.5
  133.5 2.2 copy.43
  135.8 1.5 fusion.88
  139.2 1.2 copy.39
  141.7 3.5 %copy.45 = bf16[3,192,1536]{1,0,2:T(4,128)(2,1)} copy(bf16[3,192,1536]{2,1,0:T(8,128)(2,1)S(1)} %pad_maximum_fusion.1) | data formatting | bytes 3538944
  145.3 7.0 %reshape.31 = bf16[1536,576]{1,0:T(8,128)(2,1)} reshape(bf16[1536,3,192]{2,1,0:T(4,128)(2,1)} %bitcast.98) | data formatting | bytes 3538944
  152.4 0.8 copy-done.16
  154.2 3.5 %copy.41 = bf16[3,192,1536]{1,0,2:T(4,128)(2,1)} copy(bf16[3,192,1536]{2,1,0:T(8,128)(2,1)S(1)} %pad_maximum_fusion) | data formatting | bytes 3538944
  157.8 7.1 %reshape.27 = bf16[1536,576]{1,0:T(8,128)(2,1)} reshape(bf16[1536,3,192]{2,1,0:T(4,128)(2,1)} %bitcast.99) | data formatting | bytes 3538944
  164.9 1.1 copy.48
  166.0 0.7 convert_element_type.137
  166.7 6.2 %reduce-scatter.35.cloned.1.call-done = bf16[384,192]{1,0:T(8,128)(2,1)} async-done(((bf16[1536,192]{1,0:T(8,128)(2,1)}), bf16[384,192]{1,0:T(8,128)(2,1)}) %reduce-scatter.35.cloned.1.call-update) | async-done | bytes 147472
  173.0 1.1 copy.44
  174.0 0.7 convert_element_type.133
  174.8 23.9 %reduce-scatter.31.cloned.1.call-done = bf16[384,256]{1,0:T(8,128)(2,1)} async-done(((bf16[1536,256]{1,0:T(8,128)(2,1)}), bf16[384,256]{1,0:T(8,128)(2,1)}) %reduce-scatter.31.cloned.1.call-update) | async-done | bytes 196624 | tf_op jit(solution)/shard_map/reduce_scatter | solution.py:76
  198.7 1.9 fusion.67
  200.6 41.9 %reduce-scatter.37.cloned.1.call-done = bf16[384,576]{1,0:T(8,128)(2,1)} async-done(((bf16[1536,576]{1,0:T(8,128)(2,1)}), bf16[384,576]{1,0:T(8,128)(2,1)}) %reduce-scatter.37.cloned.1.call-update) | async-done | bytes 442384
  242.5 1.8 reshape.32
  244.3 0.9 copy.46
  245.2 1.0 convert_element_type.134
  246.1 39.4 %reduce-scatter.33.cloned.1.call-done = bf16[384,576]{1,0:T(8,128)(2,1)} async-done(((bf16[1536,576]{1,0:T(8,128)(2,1)}), bf16[384,576]{1,0:T(8,128)(2,1)}) %reduce-scatter.33.cloned.1.call-update) | async-done | bytes 442384
  285.5 1.8 reshape.28
  287.3 0.9 copy.42
  288.2 1.0 convert_element_type.131
  (79 shorter events, 11.0 us)
Async XLA Ops:
  7.2 62.5 %copy-start = (bf16[1536,192]{0,1:T(8,128)(2,1)S(1)}, bf16[1536,192]{0,1:T(8,128)(2,1)}, u32[]{:S(2)}) copy-start(bf16[1536,192]{0,1:T(8,128)(2,1)} %param.10) | copy-start | bytes 1769476
  7.2 13.4 %copy-start.2 = (bf16[3,192,1536]{2,1,0:T(8,128)(2,1)S(1)}, bf16[3,192,1536]{2,1,0:T(8,128)(2,1)}, u32[]{:S(2)}) copy-start(bf16[3,192,1536]{2,1,0:T(8,128)(2,1)} %param.7) | copy-start | bytes 5308420
  7.2 40.4 %reduce-scatter.25.cloned.1.call-start = ((), (), s32[]{:S(2)}) async-start(), calls=%async_computation.9 | async-start | bytes 983040 | tf_op jit(solution)/shard_map/reduce_scatter | solution.py:46
  18.5 2.1 collective-permute-start
  20.6 1.1 copy-start.12
  21.7 25.9 %copy-start.5 = (bf16[384,256]{1,0:T(8,128)(2,1)S(1)}, bf16[384,256]{1,0:T(8,128)(2,1)}, u32[]{:S(2)}) copy-start(bf16[384,256]{1,0:T(8,128)(2,1)} %param.6) | copy-start | bytes 589828
  22.1 36.3 %copy-start.17 = (bf16[2,48,1024]{2,1,0:T(8,128)(2,1)S(1)}, bf16[2,48,1024]{2,1,0:T(8,128)(2,1)}, u32[]{:S(2)}) copy-start(bf16[2,48,1024]{2,1,0:T(8,128)(2,1)} %param.11) | copy-start | bytes 589828
  56.9 9.4 %collective-permute-start.1 = (bf16[1536,256]{1,0:T(8,128)(2,1)S(1)}, bf16[1536,256]{1,0:T(8,128)(2,1)}, u32[]{:S(2)}, u32[]{:S(2)}) collective-permute-start(bf16[1536,256]{1,0:T(8,128)(2,1)S(1)} %all_gather.13), channel_id=1, source_target_pairs={} | collective-permute-start | bytes 2359304 | tf_op jit(solution)/shard_map/ppermute | solution.py:13
  60.3 12.7 %all-to-all-start = ((bf16[4,2,12288]{2,1,0:T(2,128)(2,1)}), bf16[4,2,12288]{2,1,0:T(2,128)(2,1)}, u32[]{:S(2)}, u32[]{:S(2)}) async-start(bf16[4,2,12288]{2,1,0:T(2,128)(2,1)} %reshape.35), calls=%async_computation | async-start | bytes 393216 | tf_op jit(solution)/shard_map/all_to_all | solution.py:108
  64.9 30.6 %reduce-scatter.27.cloned.1.call-start = ((), (), s32[]{:S(2)}) async-start(), calls=%async_computation.10 | async-start | bytes 983040 | tf_op jit(solution)/shard_map/reduce_scatter | solution.py:46
  71.2 50.7 %reduce-scatter.29.cloned.1.call-start = ((), (), s32[]{:S(2)}) async-start(), calls=%async_computation.11 | async-start | bytes 983040 | tf_op jit(solution)/shard_map/reduce_scatter | solution.py:76
  74.9 9.7 %copy-start.1 = (bf16[3,192,1536]{2,1,0:T(8,128)(2,1)S(1)}, bf16[3,192,1536]{2,1,0:T(8,128)(2,1)}, u32[]{:S(2)}) copy-start(bf16[3,192,1536]{2,1,0:T(8,128)(2,1)} %param.9) | copy-start | bytes 5308420
  74.9 0.7 copy-start.8
  83.6 1.4 copy-start.4
  83.9 1.1 copy-start.13
  83.9 1.1 collective-permute-start.2
  85.0 0.6 copy-start.10
  87.3 34.7 %copy-start.9 = (bf16[2,4,48,256]{3,2,1,0:T(8,128)(2,1)S(1)}, bf16[2,4,48,256]{3,2,1,0:T(8,128)(2,1)}, u32[]{:S(2)}) copy-start(bf16[2,4,48,256]{3,2,1,0:T(8,128)(2,1)} %copy-done.8) | copy-start | bytes 589828
  87.3 77.6 %reduce-scatter.39.cloned.1.call-start = ((), (), s32[]{:S(2)}) async-start(), calls=%async_computation.16 | async-start | bytes 983040
  90.2 82.8 %reduce-scatter.35.cloned.1.call-start = ((), (), s32[]{:S(2)}) async-start(), calls=%async_computation.14 | async-start | bytes 983040
  124.1 11.7 %copy-start.6 = (bf16[384,256]{1,0:T(8,128)(2,1)}, bf16[384,256]{1,0:T(8,128)(2,1)S(1)}, u32[]{:S(2)}) copy-start(bf16[384,256]{1,0:T(8,128)(2,1)S(1)} %get-tuple-element.24) | copy-start | bytes 589828
  135.7 62.9 %reduce-scatter.31.cloned.1.call-start = ((), (), s32[]{:S(2)}) async-start(), calls=%async_computation.12 | async-start | bytes 983040 | tf_op jit(solution)/shard_map/reduce_scatter | solution.py:76
  135.8 2.2 copy-start.3
  137.3 1.5 copy-start.15
  137.3 1.1 collective-permute-start.3
  139.2 1.4 copy-start.14
  139.2 1.9 copy-start.11
  140.4 102.1 %reduce-scatter.37.cloned.1.call-start = ((), (), s32[]{:S(2)}) async-start(), calls=%async_computation.15 | async-start | bytes 2457600
  152.3 0.9 copy-start.16
  152.3 133.2 %reduce-scatter.33.cloned.1.call-start = ((), (), s32[]{:S(2)}) async-start(), calls=%async_computation.13 | async-start | bytes 2457600
  164.8 33.8 %copy-start.7 = (bf16[384,256]{1,0:T(8,128)(2,1)S(1)}, bf16[384,256]{1,0:T(8,128)(2,1)}, u32[]{:S(2)}) copy-start(bf16[384,256]{1,0:T(8,128)(2,1)} %copy-done.6) | copy-start | bytes 589828
Sparse Core Ops, SparseCore 0:
  23.4 24.1 reduce-scatter.24
  71.4 24.1 reduce-scatter.26
  98.6 23.2 reduce-scatter.28
  124.2 23.3 reduce-scatter.38
  150.4 22.5 reduce-scatter.34
  176.1 22.5 reduce-scatter.30
  201.0 41.4 reduce-scatter.36
  244.8 40.6 reduce-scatter.32
where the time goes:
time: 297 us; the launch traced here: 296 us
  waiting for transfers between devices  169 us (57%)
  local copies, waits for them, and re-layouts  42.7 us (14%)
  blocking collectives  34.5 us (12%)
  matrix products  16.2 us (5%)
  between operations  14.6 us (5%)
  other arithmetic  10.2 us (3%)
  starting transfers between devices  8.6 us (3%)
    unnamed x12, waiting for transfers between devices  87.6 us
    reduce_scatter x2, waiting for transfers between devices, residual_block_backward(): lax.psum_scatter((total + contract_first(conv_weight[2], moved[2])).astyp...  50.3 us
    unnamed x55, local copies, waits for them, and re-layouts  42.3 us
    reduce_scatter x2, waiting for transfers between devices, residual_block_forward(): lax.psum_scatter(jnp.dot(point_weight, hidden, preferred_element_type=jnp...  29.6 us
    all_gather x2, blocking collectives, residual_block_forward(): squashed = lax.all_gather(squash_part, 'mp', axis=0, tiled=True)  18.3 us
    all_gather x2, blocking collectives, residual_block_backward(): upstream_full = lax.all_gather(incoming_gradient, 'mp', axis=0, tiled=True)  16.2 us
  transfers between devices with their start and end apart: 13, of which 8 were waited for; matrix products, arithmetic and copies ran while one was open for 20% of the time, Pallas kernels for 0%

commit v1 on v0

--- a/solution.py
+++ b/solution.py
@@ -1,6 +1,10 @@
+import functools
+
 import jax
 import jax.numpy as jnp
 from jax import lax
+from jax.experimental import pallas as pl
+from jax.experimental.pallas import tpu as pltpu
 from jax.sharding import PartitionSpec as P
 
 FIRST_DILATION = 1024
@@ -151,6 +155,360 @@
     )
 
 
+GELU_SCALE = 0.7978845608028654
+GELU_CUBIC = 0.044715
+
+
+def gelu_of(s):
+    return 0.5 * s * (1.0 + jnp.tanh(GELU_SCALE * (s + GELU_CUBIC * (s * s * s))))
+
+
+def slope_of(s):
+    t = jnp.tanh(GELU_SCALE * (s + GELU_CUBIC * (s * s * s)))
+    inner = GELU_SCALE * (1.0 + 3.0 * GELU_CUBIC * (s * s))
+    return 0.5 * (1.0 + t) + 0.5 * s * (1.0 - t * t) * inner
+
+
+def whole_kernel(
+    n,
+    x_h, k1_h, p1_h, k2_h, p2_h, g_h,
+    out_o, gx_o, gk1_o, gp1_o, gk2_o, gp2_o,
+    x_v, mid_v, k1, p1, k2, p2, z1, z2, g2, g1, u1, u2, v1, v2, gu1, gu2, gh,
+    rs_out, rs_in, part, from_left, from_right,
+    send, recv, load,
+):
+    rows, bins = x_v.shape
+    chans = z1.shape[0]
+    heads, vals = g_h.shape[0], g_h.shape[1]
+    c, m = lax.axis_index("ctx"), lax.axis_index("mp")
+    sib = m + 1 - 2 * (m % 2)
+    cross = (m + 2) % 4
+    far = 3 - m
+    f32, bf16 = jnp.float32, jnp.bfloat16
+    counter = iter(range(send.shape[0]))
+    sent = []
+
+    def remote(src, dst, i, **device):
+        return pltpu.make_async_remote_copy(
+            src_ref=src,
+            dst_ref=dst,
+            send_sem=send.at[i],
+            recv_sem=recv.at[i],
+            device_id=device,
+            device_id_type=pl.DeviceIdType.MESH,
+        )
+
+    def start(copy):
+        copy.start()
+        sent.append(copy)
+
+    loads = [
+        pltpu.make_async_copy(src, dst, load.at[i])
+        for i, (src, dst) in enumerate(
+            ((x_h, x_v), (k1_h.at[1], k1), (p1_h, p1), (p2_h, p2), (k2_h.at[1], k2))
+        )
+    ]
+    for copy in loads:
+        copy.start()
+
+    def grad_rows(owner, h):
+        return pl.ds(pl.multiple_of(h * vals * n + owner * vals, 16), vals)
+
+    def grad_bins(owner):
+        return pl.ds(pl.multiple_of(owner * bins, 128), bins)
+
+    own_grad = [
+        pltpu.make_async_copy(
+            g_h.at[h, :, grad_bins(c)], g2.at[m, grad_rows(c, h), :], load.at[5 + h]
+        )
+        for h in range(heads)
+    ]
+    for copy in own_grad:
+        copy.start()
+
+    barrier = pltpu.get_barrier_semaphore()
+    for k in range(1, n):
+        pl.semaphore_signal(
+            barrier, inc=1, device_id={"ctx": (c + k) % n}, device_id_type=pl.DeviceIdType.MESH
+        )
+    for peer in (sib, cross):
+        pl.semaphore_signal(
+            barrier, inc=1, device_id={"mp": peer}, device_id_type=pl.DeviceIdType.MESH
+        )
+
+    def gather_start(buf):
+        ids = [next(counter) for _ in range(3)]
+        start(remote(buf.at[m], buf.at[m], ids[0], mp=cross))
+        start(remote(buf.at[m], buf.at[m], ids[1], mp=sib))
+        return ids
+
+    def gather_forward(buf, ids):
+        remote(buf.at[cross], buf.at[cross], ids[0], mp=cross).wait_recv()
+        start(remote(buf.at[cross], buf.at[cross], ids[2], mp=sib))
+
+    def gather_end(buf, ids):
+        remote(buf.at[sib], buf.at[sib], ids[1], mp=sib).wait_recv()
+        remote(buf.at[far], buf.at[far], ids[2], mp=sib).wait_recv()
+
+    def scatter_start(i, block_of):
+        ids = [next(counter) for _ in range(3)]
+        for slot, block in ((0, far), (1, sib)):
+            rs_out[i, slot] = block_of(block).astype(bf16)
+            start(remote(rs_out.at[i, slot], rs_in.at[i, slot], ids[slot], mp=sib))
+        return ids
+
+    def scatter_cross(i, ids, block_of):
+        term = block_of(cross)
+        remote(rs_out.at[i, 0], rs_in.at[i, 0], ids[0], mp=sib).wait_recv()
+        rs_out[i, 2] = (term + rs_in[i, 0].astype(f32)).astype(bf16)
+        start(remote(rs_out.at[i, 2], rs_in.at[i, 2], ids[2], mp=cross))
+
+    def scatter_end(i, ids, block_of):
+        term = block_of(m)
+        remote(rs_out.at[i, 1], rs_in.at[i, 1], ids[1], mp=sib).wait_recv()
+        term = term + rs_in[i, 1].astype(f32)
+        remote(rs_out.at[i, 2], rs_in.at[i, 2], ids[2], mp=cross).wait_recv()
+        return term + rs_in[i, 2].astype(f32)
+
+    line_ids = [[(next(counter), next(counter)) for _ in range(n)] for _ in range(4)]
+
+    def to_right(i, d):
+        peer = jnp.minimum(c + 1, n - 1)
+        return remote(part.at[i, d], from_left.at[i, d], line_ids[i][d][0], ctx=peer)
+
+    def to_left(i, d):
+        peer = jnp.maximum(c - 1, 0)
+        return remote(part.at[i, d], from_right.at[i, d], line_ids[i][d][1], ctx=peer)
+
+    def line_first(i):
+        for d in range(n - 1, 0, -1):
+
+            @pl.when(c == 0)
+            def _():
+                to_right(i, d).start()
+
+            @pl.when(c == n - 1)
+            def _():
+                to_left(i, n - 1 - d).start()
+
+    def line_relay(i):
+        for d in range(n - 1, 0, -1):
+
+            @pl.when((c > 0) & (c < d))
+            def _():
+                right = to_right(i, d)
+                right.wait_recv()
+                part[i, d] = (part[i, d].astype(f32) + from_left[i, d].astype(f32)).astype(bf16)
+                right.start()
+
+            @pl.when((c < n - 1) & (c > n - 1 - d))
+            def _():
+                e = n - 1 - d
+                left = to_left(i, e)
+                left.wait_recv()
+                part[i, e] = (part[i, e].astype(f32) + from_right[i, e].astype(f32)).astype(bf16)
+                left.start()
+
+    def line_end(i, result):
+        for d in range(n):
+
+            @pl.when(c == d)
+            def _():
+                total = part[i, d].astype(f32)
+                if d > 0:
+                    to_right(i, d).wait_recv()
+                    total = total + from_left[i, d].astype(f32)
+                if d < n - 1:
+                    to_left(i, d).wait_recv()
+                    total = total + from_right[i, d].astype(f32)
+                result[...] = total
+
+    def line_drain(i):
+        for d in range(n):
+
+            @pl.when(c < d)
+            def _():
+                to_right(i, d).wait_send()
+
+            @pl.when(c > d)
+            def _():
+                to_left(i, d).wait_send()
+
+    def dot(a, b, left, right):
+        return lax.dot_general(
+            a, b, (((left,), (right,)), ((), ())), preferred_element_type=f32
+        )
+
+    def block_rows(b):
+        return pl.ds(pl.multiple_of(b * rows, 128), rows)
+
+    def mixed(p, v):
+        return lambda b: dot(p[block_rows(b), :], v[...], 1, 0)
+
+    def spread(k, gu):
+        return lambda b: dot(k[:, block_rows(b)], gu[...], 0, 0)
+
+    def flat(buf):
+        return buf[...].reshape(chans * rows, bins)
+
+    def products(i, left, right):
+        for d in range(n):
+            part[i, d] = dot(left[...], right[d], 1, 1).astype(bf16)
+
+    loads[0].wait()
+    z1[m] = gelu_of(x_v[...].astype(f32)).astype(bf16)
+    pl.semaphore_wait(barrier, n + 1)
+    z1_ids = gather_start(z1)
+    grad_ids = [[next(counter) for _ in range(heads)] for _ in range(n)]
+    for k in range(1, n):
+        peer = (c + k) % n
+        for h in range(heads):
+            start(
+                remote(
+                    g_h.at[h, :, grad_bins(peer)],
+                    g2.at[m, grad_rows(c, h), :],
+                    grad_ids[k][h],
+                    ctx=peer,
+                )
+            )
+    gather_forward(z1, z1_ids)
+    for copy in loads[1:]:
+        copy.wait()
+    gather_end(z1, z1_ids)
+    u1[...] = dot(k1[...], flat(z1), 1, 0)
+    v1[...] = gelu_of(u1[...]).astype(bf16)
+    mixed1 = mixed(p1, v1)
+    rs_ids = scatter_start(0, mixed1)
+    for copy in own_grad:
+        copy.wait()
+    for k in range(1, n):
+        origin = (c + n - k) % n
+        for h in range(heads):
+            remote(
+                g_h.at[h, :, grad_bins(origin)],
+                g2.at[m, grad_rows(origin, h), :],
+                grad_ids[k][h],
+                ctx=origin,
+            ).wait_recv()
+    g2_ids = gather_start(g2)
+    scatter_cross(0, rs_ids, mixed1)
+    gather_forward(g2, g2_ids)
+    middle = x_v[...].astype(f32) + scatter_end(0, rs_ids, mixed1)
+    mid_v[...] = middle.astype(bf16)
+    z2[m] = gelu_of(mid_v[...].astype(f32)).astype(bf16)
+    z2_ids = gather_start(z2)
+    gather_end(g2, g2_ids)
+    gh[...] = dot(p2[...], flat(g2), 0, 0)
+    gather_forward(z2, z2_ids)
+    gather_end(z2, z2_ids)
+    u2[...] = dot(k2[...], flat(z2), 1, 0)
+    v2[...] = gelu_of(u2[...]).astype(bf16)
+    gu2[...] = (gh[...] * slope_of(u2[...])).astype(bf16)
+    spread2 = spread(k2, gu2)
+    rs_ids = scatter_start(1, spread2)
+    products(0, v2, g2)
+    line_first(0)
+    scatter_cross(1, rs_ids, spread2)
+    products(1, gu2, z2)
+    line_first(1)
+    mid_slope = slope_of(mid_v[...].astype(f32))
+    previous = g2[m].astype(f32) + scatter_end(1, rs_ids, spread2) * mid_slope
+    g1[m] = previous.astype(bf16)
+    g1_ids = gather_start(g1)
+    mixed2 = mixed(p2, v2)
+    out_ids = scatter_start(2, mixed2)
+    line_relay(0)
+    gather_forward(g1, g1_ids)
+    gather_end(g1, g1_ids)
+    gh[...] = dot(p1[...], flat(g1), 0, 0)
+    gu1[...] = (gh[...] * slope_of(u1[...])).astype(bf16)
+    spread1 = spread(k1, gu1)
+    rs_ids = scatter_start(3, spread1)
+    products(2, gu1, z1)
+    line_first(2)
+    products(3, v1, g1)
+    line_first(3)
+    scatter_cross(3, rs_ids, spread1)
+    scatter_cross(2, out_ids, mixed2)
+    line_relay(1)
+    first_slope = slope_of(x_v[...].astype(f32))
+    previous = g1[m].astype(f32) + scatter_end(3, rs_ids, spread1) * first_slope
+    gx_o[...] = previous.astype(bf16)
+    result = mid_v[...].astype(f32) + scatter_end(2, out_ids, mixed2)
+    out_o[...] = result.astype(bf16)
+    line_relay(2)
+    line_relay(3)
+    for i, result_o in enumerate((gp2_o, gk2_o, gk1_o, gp1_o)):
+        line_end(i, result_o)
+    for copy in sent:
+        copy.wait_send()
+    for i in range(4):
+        line_drain(i)
+
+
+def short_sequence(sizes, x, k1, p1, k2, p2, grad):
+    n, parts = sizes["ctx"], sizes["mp"]
+    rows, bins = x.shape
+    width = k1.shape[1]
+    bf16, f32 = jnp.bfloat16, jnp.float32
+    full = pltpu.VMEM((parts, rows, bins), bf16)
+    shares = pltpu.VMEM((4, n, width, rows), bf16)
+    copies = 24 + 8 * n + grad.shape[0] * n
+    inner = [pltpu.VMEM((width, bins), f32)] * 2 + [pltpu.VMEM((width, bins), bf16)] * 4
+    results = pl.pallas_call(
+        functools.partial(whole_kernel, n),
+        out_shape=[
+            jax.ShapeDtypeStruct((rows, bins), bf16),
+            jax.ShapeDtypeStruct((rows, bins), bf16),
+        ]
+        + [jax.ShapeDtypeStruct((width, rows), f32)] * 4,
+        in_specs=[pl.BlockSpec(memory_space=pl.ANY)] * 6,
+        out_specs=[pl.BlockSpec(memory_space=pltpu.VMEM)] * 6,
+        scratch_shapes=[
+            pltpu.VMEM((rows, bins), bf16),
+            pltpu.VMEM((rows, bins), bf16),
+            pltpu.VMEM((width, k1.shape[2]), bf16),
+            pltpu.VMEM(p1.shape, bf16),
+            pltpu.VMEM((width, k1.shape[2]), bf16),
+            pltpu.VMEM(p1.shape, bf16),
+            full, full, full, full,
+        ]
+        + inner
+        + [
+            pltpu.VMEM((width, bins), f32),
+            pltpu.VMEM((4, 3, rows, bins), bf16),
+            pltpu.VMEM((4, 3, rows, bins), bf16),
+            shares, shares, shares,
+            pltpu.SemaphoreType.DMA((copies,)),
+            pltpu.SemaphoreType.DMA((copies,)),
+            pltpu.SemaphoreType.DMA((5 + grad.shape[0],)),
+        ],
+        compiler_params=pltpu.CompilerParams(
+            collective_id=0, has_side_effects=True, vmem_limit_bytes=48 * 1024 * 1024
+        ),
+        name="blocks",
+    )(x, k1, p1, k2, p2, grad)
+    out, gx, gk1, gp1, gk2, gp2 = results
+    around = ((1, 1), (0, 0), (0, 0))
+    return (
+        out,
+        gx,
+        jnp.pad(gk1[None], around),
+        gp1.T,
+        jnp.pad(gk2[None], around),
+        gp2.T,
+    )
+
+
+def device_program(sizes, x, k1, p1, k2, p2, grad):
+    n = sizes["ctx"]
+    length = n * x.shape[1]
+    short = min(FIRST_DILATION, SECOND_DILATION) >= length
+    if short and n == 4 and sizes["mp"] == 4:
+        return short_sequence(sizes, x, k1, p1, k2, p2, grad)
+    return shards(x, k1, p1, k2, p2, grad)
+
+
 def solution(mesh):
     placed = (
         P("mp", ("groups", "ctx")),
@@ -161,7 +519,7 @@
         P("mp", "ctx", "groups"),
     )
     return jax.shard_map(
-        shards,
+        functools.partial(device_program, dict(mesh.shape)),
         mesh=mesh,
         in_specs=placed,
         out_specs=(

time: 297 us -> 99.3 us (0.33)
  waiting for transfers between devices: 169 us -> 0 us
  Pallas kernels: 0 us -> 90 us
  blocking collectives: 34.5 us -> 0 us
  local copies, waits for them, and re-layouts: 42.7 us -> 8.46 us
  matrix products: 16.2 us -> 0 us
  between operations: 14.6 us -> 0.69 us
  other arithmetic: 10.2 us -> 0 us
  starting transfers between devices: 8.6 us -> 0 us
    pallas_call x0 -> x1, Pallas kernels: none -> 90 us  [short_sequence(): pl.pallas_call(functools.partial(whole_kernel, n), out_shape=[jax.ShapeDt...]
    unnamed x12 -> x0, waiting for transfers between devices: 87.6 us -> none
    reduce_scatter x4 -> x0, waiting for transfers between devices: 79.9 us -> none  [the longest x2 50.3 us: residual_block_backward(): lax.psum_scatter((total + contract_first(conv_weight[2], moved[2])).astyp...]
    unnamed x55 -> x12, local copies, waits for them, and re-layouts: 42.3 us -> 6.52 us
    all_gather x4 -> x0, blocking collectives: 34.5 us -> none  [the longest x2 18.3 us: residual_block_forward(): squashed = lax.all_gather(squash_part, 'mp', axis=0, tiled=True)]
    dot_general x22 -> x0, matrix products: 16.2 us -> none  [the longest x6 4.55 us: contract_last(): lax.dot_general(left, right, (((1,), (1,)), ((), ())), preferred_element_...]
    convert_element_type x8 -> x0, other arithmetic: 9.77 us -> none  [the longest x2 4.03 us: residual_block_backward(): previous = (incoming_gradient.astype(jnp.float32) + grad_squash * gelu_sl...]
    all_to_all x1 -> x0, starting transfers between devices: 4.59 us -> none  [shards(): lax.all_to_all(grad_heads, 'ctx', split_axis=2, concat_axis=1, tiled=True)]
  transfers between devices with their start and end apart: 13 -> 0, of which waited for: 8 -> 0; matrix products, arithmetic and copies ran while one was open for 20% -> 0% of each run, Pallas kernels for 0% -> 0%
where the time goes in v1:
time: 99.3 us; the launch traced here: 99.1 us
  Pallas kernels  90 us (91%)
  local copies, waits for them, and re-layouts  8.46 us (9%)
    pallas_call x1, Pallas kernels, short_sequence(): pl.pallas_call(functools.partial(whole_kernel, n), out_shape=[jax.ShapeDt...  90 us
    unnamed x12, local copies, waits for them, and re-layouts  6.52 us

profile of v1, /device:TPU:0, one launch (start us, length us, event | category | flops | bytes accessed | tf_op | source)
XLA Modules:
  0.0 99.1 jit_solution(15744899485065654486)
XLA Ops:
  0.6 0.0 copy-start
  0.6 0.0 copy-start.1
  0.7 1.5 %copy.12.p1_h = bf16[1536,192]{1,0:T(8,128)(2,1)S(1)} copy(bf16[1536,192]{0,1:T(8,128)(2,1)} %param.8) | data formatting | bytes 1179648 | tf_op args[2]
  2.1 1.3 %copy.13.p2_h = bf16[1536,192]{1,0:T(8,128)(2,1)S(1)} copy(bf16[1536,192]{0,1:T(8,128)(2,1)} %param.10) | data formatting | bytes 1179648 | tf_op args[4]
  3.5 0.0 copy-done
  3.5 0.0 copy-done.1
  3.5 0.0 copy-start.2
  3.5 0.9 copy-done.2
  4.4 90.0 %blocks.1 = (bf16[384,256]{1,0:T(8,128)(2,1)S(1)}, bf16[384,256]{1,0:T(8,128)(2,1)S(1)}, f32[192,384]{1,0:T(8,128)S(1)}, f32[192,384]{1,0:T(8,128)S(1)}, f32[192,384]{1,0:T(8,128)S(1)}, /*index=5*/f32[192,384]{1,0:T(8,128)S(1)}) custom-call(bf16[384,256]{1,0:T(8,128)(2,1)S(1)} %copy-done.1, bf16[3,192,1536]{2,1,0:T(8,128)(2,1)S(1)} %copy-done, ...), custom_call_target="tpu_custom_call" | custom-call | tf_op jit(solution)/shard_map/blocks/pallas_call | solution.py:458
  94.4 1.0 pad.7
  95.4 1.0 pad.8
  96.3 0.7 copy.18
  97.0 0.7 copy.19
  97.7 0.7 copy.20
  98.4 0.7 copy.21
Async XLA Ops:
  0.6 2.8 %copy-start = (bf16[3,192,1536]{2,1,0:T(8,128)(2,1)S(1)}, bf16[3,192,1536]{2,1,0:T(8,128)(2,1)}, u32[]{:S(2)}) copy-start(bf16[3,192,1536]{2,1,0:T(8,128)(2,1)} %k1_h.1) | copy-start | bytes 5308420
  0.6 2.8 %copy-start.1 = (bf16[384,256]{1,0:T(8,128)(2,1)S(1)}, bf16[384,256]{1,0:T(8,128)(2,1)}, u32[]{:S(2)}) copy-start(bf16[384,256]{1,0:T(8,128)(2,1)} %x_h.1) | copy-start | bytes 589828
  3.5 0.9 copy-start.2

commit v2 on v1

--- a/solution.py
+++ b/solution.py
@@ -280,34 +280,35 @@
         peer = jnp.maximum(c - 1, 0)
         return remote(part.at[i, d], from_right.at[i, d], line_ids[i][d][1], ctx=peer)
 
-    def line_first(i):
+    def line_first(*grads):
         for d in range(n - 1, 0, -1):
-
-            @pl.when(c == 0)
+            for i in grads:
+
+                @pl.when(c == 0)
+                def _():
+                    to_right(i, d).start()
+
+                @pl.when(c == n - 1)
+                def _():
+                    to_left(i, n - 1 - d).start()
+
+    def line_relay(i, hop):
+        for d in range(n - 1, hop, -1):
+
+            @pl.when(c == hop)
             def _():
-                to_right(i, d).start()
-
-            @pl.when(c == n - 1)
-            def _():
-                to_left(i, n - 1 - d).start()
-
-    def line_relay(i):
-        for d in range(n - 1, 0, -1):
-
-            @pl.when((c > 0) & (c < d))
-            def _():
-                right = to_right(i, d)
-                right.wait_recv()
+                copy = to_right(i, d)
+                copy.wait_recv()
                 part[i, d] = (part[i, d].astype(f32) + from_left[i, d].astype(f32)).astype(bf16)
-                right.start()
-
-            @pl.when((c < n - 1) & (c > n - 1 - d))
+                copy.start()
+
+            @pl.when(c == n - 1 - hop)
             def _():
                 e = n - 1 - d
-                left = to_left(i, e)
-                left.wait_recv()
+                copy = to_left(i, e)
+                copy.wait_recv()
                 part[i, e] = (part[i, e].astype(f32) + from_right[i, e].astype(f32)).astype(bf16)
-                left.start()
+                copy.start()
 
     def line_end(i, result):
         for d in range(n):
@@ -343,7 +344,7 @@
         return pl.ds(pl.multiple_of(b * rows, 128), rows)
 
     def mixed(p, v):
-        return lambda b: dot(p[block_rows(b), :], v[...], 1, 0)
+        return lambda b: dot(p[:, block_rows(b)], v[...], 0, 0)
 
     def spread(k, gu):
         return lambda b: dot(k[:, block_rows(b)], gu[...], 0, 0)
@@ -398,7 +399,7 @@
     z2[m] = gelu_of(mid_v[...].astype(f32)).astype(bf16)
     z2_ids = gather_start(z2)
     gather_end(g2, g2_ids)
-    gh[...] = dot(p2[...], flat(g2), 0, 0)
+    gh[...] = dot(p2[...], flat(g2), 1, 0)
     gather_forward(z2, z2_ids)
     gather_end(z2, z2_ids)
     u2[...] = dot(k2[...], flat(z2), 1, 0)
@@ -407,43 +408,53 @@
     spread2 = spread(k2, gu2)
     rs_ids = scatter_start(1, spread2)
     products(0, v2, g2)
-    line_first(0)
+    products(1, gu2, z2)
+    line_first(0, 1)
     scatter_cross(1, rs_ids, spread2)
-    products(1, gu2, z2)
-    line_first(1)
     mid_slope = slope_of(mid_v[...].astype(f32))
+    mixed2 = mixed(p2, v2)
+    out_ids = scatter_start(2, mixed2)
     previous = g2[m].astype(f32) + scatter_end(1, rs_ids, spread2) * mid_slope
     g1[m] = previous.astype(bf16)
     g1_ids = gather_start(g1)
-    mixed2 = mixed(p2, v2)
-    out_ids = scatter_start(2, mixed2)
-    line_relay(0)
+    line_relay(0, 1)
     gather_forward(g1, g1_ids)
     gather_end(g1, g1_ids)
-    gh[...] = dot(p1[...], flat(g1), 0, 0)
+    gh[...] = dot(p1[...], flat(g1), 1, 0)
     gu1[...] = (gh[...] * slope_of(u1[...])).astype(bf16)
     spread1 = spread(k1, gu1)
     rs_ids = scatter_start(3, spread1)
     products(2, gu1, z1)
-    line_first(2)
     products(3, v1, g1)
-    line_first(3)
+    line_first(2, 3)
+    line_relay(1, 1)
+    for i in (0, 1):
+        for hop in range(2, n - 1):
+            line_relay(i, hop)
     scatter_cross(3, rs_ids, spread1)
     scatter_cross(2, out_ids, mixed2)
-    line_relay(1)
     first_slope = slope_of(x_v[...].astype(f32))
     previous = g1[m].astype(f32) + scatter_end(3, rs_ids, spread1) * first_slope
     gx_o[...] = previous.astype(bf16)
     result = mid_v[...].astype(f32) + scatter_end(2, out_ids, mixed2)
     out_o[...] = result.astype(bf16)
-    line_relay(2)
-    line_relay(3)
+    for hop in range(1, n - 1):
+        for i in (2, 3):
+            line_relay(i, hop)
     for i, result_o in enumerate((gp2_o, gk2_o, gk1_o, gp1_o)):
         line_end(i, result_o)
     for copy in sent:
         copy.wait_send()
     for i in range(4):
         line_drain(i)
+
+
+def write_results(out_i, gx_i, gk1_i, gp1_i, gk2_i, gp2_i, out_o, gx_o, gk1_o, gp1_o, gk2_o, gp2_o):
+    for taken, given in ((out_i, out_o), (gx_i, gx_o), (gp1_i, gp1_o), (gp2_i, gp2_o)):
+        given[...] = taken[...]
+    for taken, given in ((gk1_i, gk1_o), (gk2_i, gk2_o)):
+        given[...] = jnp.zeros_like(given)
+        given[1] = taken[...]
 
 
 def short_sequence(sizes, x, k1, p1, k2, p2, grad):
@@ -468,9 +479,9 @@
             pltpu.VMEM((rows, bins), bf16),
             pltpu.VMEM((rows, bins), bf16),
             pltpu.VMEM((width, k1.shape[2]), bf16),
-            pltpu.VMEM(p1.shape, bf16),
+            pltpu.VMEM(p1.shape[::-1], bf16),
             pltpu.VMEM((width, k1.shape[2]), bf16),
-            pltpu.VMEM(p1.shape, bf16),
+            pltpu.VMEM(p1.shape[::-1], bf16),
             full, full, full, full,
         ]
         + inner
@@ -484,20 +495,24 @@
             pltpu.SemaphoreType.DMA((5 + grad.shape[0],)),
         ],
         compiler_params=pltpu.CompilerParams(
-            collective_id=0, has_side_effects=True, vmem_limit_bytes=48 * 1024 * 1024
+            collective_id=0, has_side_effects=True, vmem_limit_bytes=56 * 1024 * 1024
         ),
         name="blocks",
-    )(x, k1, p1, k2, p2, grad)
-    out, gx, gk1, gp1, gk2, gp2 = results
-    around = ((1, 1), (0, 0), (0, 0))
-    return (
-        out,
-        gx,
-        jnp.pad(gk1[None], around),
-        gp1.T,
-        jnp.pad(gk2[None], around),
-        gp2.T,
-    )
+    )(x, k1, p1.T, k2, p2.T, grad)
+    taps = jax.ShapeDtypeStruct((k1.shape[0], width, rows), f32)
+    points = jax.ShapeDtypeStruct((width, rows), f32)
+    out, gx, gk1, gp1, gk2, gp2 = pl.pallas_call(
+        write_results,
+        out_shape=[
+            jax.ShapeDtypeStruct((rows, bins), bf16),
+            jax.ShapeDtypeStruct((rows, bins), bf16),
+            taps, points, taps, points,
+        ],
+        in_specs=[pl.BlockSpec(memory_space=pltpu.VMEM)] * 6,
+        out_specs=[pl.BlockSpec(memory_space=pltpu.VMEM)] * 6,
+        name="results",
+    )(*results)
+    return out, gx, gk1, gp1.T, gk2, gp2.T
 
 
 def device_program(sizes, x, k1, p1, k2, p2, grad):

time: 99.3 us -> 85.4 us (0.86)
  local copies, waits for them, and re-layouts: 8.46 us -> 0 us
  Pallas kernels: 90 us -> 84.6 us
    pallas_call x1, Pallas kernels: 90 us -> 81.6 us  [short_sequence(): pl.pallas_call(functools.partial(whole_kernel, n), out_shape=[jax.ShapeDt...]
    unnamed x12 -> x0, local copies, waits for them, and re-layouts: 6.52 us -> none
    pallas_call x0 -> x1, Pallas kernels: none -> 3.05 us  [short_sequence(): pl.pallas_call(write_results, out_shape=[jax.ShapeDtypeStruct((rows, bins...]
    pad x2 -> x0, local copies, waits for them, and re-layouts: 1.94 us -> none  [the longest x1 0.97 us: short_sequence(): jnp.pad(gk1[None], around)]
where the time goes in v2:
time: 85.4 us; the launch traced here: 85.3 us
  Pallas kernels  84.6 us (99%)
    pallas_call x1, Pallas kernels, short_sequence(): pl.pallas_call(functools.partial(whole_kernel, n), out_shape=[jax.ShapeDt...  81.6 us
    pallas_call x1, Pallas kernels, short_sequence(): pl.pallas_call(write_results, out_shape=[jax.ShapeDtypeStruct((rows, bins...  3.05 us

profile of v2, /device:TPU:0, one launch (start us, length us, event | category | flops | bytes accessed | tf_op | source)
XLA Modules:
  0.0 85.3 jit_solution(16970111142389344265)
XLA Ops:
  0.6 81.6 %blocks.1 = (bf16[384,256]{1,0:T(8,128)(2,1)}, bf16[384,256]{1,0:T(8,128)(2,1)}, f32[192,384]{1,0:T(8,128)}, f32[192,384]{1,0:T(8,128)}, f32[192,384]{1,0:T(8,128)}, /*index=5*/f32[192,384]{1,0:T(8,128)}) custom-call(bf16[384,256]{1,0:T(8,128)(2,1)} %x_h.1, bf16[3,192,1536]{2,1,0:T(8,128)(2,1)} %k1_h.1, bf16[192,1536]{1,0:T(8,128)(2,1)} %bitcast.4, ...), custom_call_target="tpu_custom_call" | custom-call | tf_op jit(solution)/shard_map/blocks/pallas_call | solution.py:469
  82.2 3.0 %results.1 = (bf16[384,256]{1,0:T(8,128)(2,1)}, bf16[384,256]{1,0:T(8,128)(2,1)}, f32[3,192,384]{2,1,0:T(8,128)}, f32[192,384]{1,0:T(8,128)}, f32[3,192,384]{2,1,0:T(8,128)}, /*index=5*/f32[192,384]{1,0:T(8,128)}) custom-call(bf16[384,256]{1,0:T(8,128)(2,1)} %get-tuple-element.18.out_i, bf16[384,256]{1,0:T(8,128)(2,1)} %get-tuple-element.19.gx_i, ...), custom_call_target="tpu_custom_call" | custom-call | tf_op jit(solution)/shard_map/results/pallas_call | solution.py:504

commit v3 on v2

--- a/solution.py
+++ b/solution.py
@@ -173,7 +173,8 @@
     n,
     x_h, k1_h, p1_h, k2_h, p2_h, g_h,
     out_o, gx_o, gk1_o, gp1_o, gk2_o, gp2_o,
-    x_v, mid_v, k1, p1, k2, p2, z1, z2, g2, g1, u1, u2, v1, v2, gu1, gu2, gh,
+    x_v, mid_v, k1, p1, k2, p2, z1, z2, g2, g1, u1, u2, gh, v2, gu2,
+    v_all, gu_all, z_rows, g_rows,
     rs_out, rs_in, part, from_left, from_right,
     send, recv, load,
 ):
@@ -236,19 +237,48 @@
             barrier, inc=1, device_id={"mp": peer}, device_id_type=pl.DeviceIdType.MESH
         )
 
-    def gather_start(buf):
-        ids = [next(counter) for _ in range(3)]
-        start(remote(buf.at[m], buf.at[m], ids[0], mp=cross))
-        start(remote(buf.at[m], buf.at[m], ids[1], mp=sib))
+    def pieces(buf):
+        return [lambda b: buf.at[b]]
+
+    def gather_start(views):
+        ids = []
+        for view in views:
+            own = [next(counter) for _ in range(3)]
+            start(remote(view(m), view(m), own[0], mp=cross))
+            start(remote(view(m), view(m), own[1], mp=sib))
+            ids.append(own)
         return ids
 
-    def gather_forward(buf, ids):
-        remote(buf.at[cross], buf.at[cross], ids[0], mp=cross).wait_recv()
-        start(remote(buf.at[cross], buf.at[cross], ids[2], mp=sib))
-
-    def gather_end(buf, ids):
-        remote(buf.at[sib], buf.at[sib], ids[1], mp=sib).wait_recv()
-        remote(buf.at[far], buf.at[far], ids[2], mp=sib).wait_recv()
+    def gather_forward(views, ids):
+        for view, own in zip(views, ids):
+            remote(view(cross), view(cross), own[0], mp=cross).wait_recv()
+            start(remote(view(cross), view(cross), own[2], mp=sib))
+
+    def gather_end(views, ids):
+        for view, own in zip(views, ids):
+            remote(view(sib), view(sib), own[1], mp=sib).wait_recv()
+            remote(view(far), view(far), own[2], mp=sib).wait_recv()
+
+    def push_start(source, target):
+        ids = [next(counter) for _ in range(n)]
+        for k in range(1, n):
+            peer = (c + k) % n
+            start(remote(source(peer), target(c), ids[k], ctx=peer))
+        return ids
+
+    def push_wait(target, ids):
+        for k in range(1, n):
+            origin = (c + n - k) % n
+            remote(target(origin), target(origin), ids[k], ctx=origin).wait_recv()
+
+    def quarter(b):
+        return pl.ds(pl.multiple_of(b * (rows // 4), 16), rows // 4)
+
+    def row_views(buf):
+        def view_of(k):
+            return lambda b: buf.at[(c + k) % n, quarter(b), :]
+
+        return [view_of(k) for k in range(1, n)]
 
     def scatter_start(i, block_of):
         ids = [next(counter) for _ in range(3)]
@@ -270,7 +300,7 @@
         remote(rs_out.at[i, 2], rs_in.at[i, 2], ids[2], mp=cross).wait_recv()
         return term + rs_in[i, 2].astype(f32)
 
-    line_ids = [[(next(counter), next(counter)) for _ in range(n)] for _ in range(4)]
+    line_ids = [[(next(counter), next(counter)) for _ in range(n)] for _ in range(2)]
 
     def to_right(i, d):
         peer = jnp.minimum(c + 1, n - 1)
@@ -359,7 +389,7 @@
     loads[0].wait()
     z1[m] = gelu_of(x_v[...].astype(f32)).astype(bf16)
     pl.semaphore_wait(barrier, n + 1)
-    z1_ids = gather_start(z1)
+    z1_ids = gather_start(pieces(z1))
     grad_ids = [[next(counter) for _ in range(heads)] for _ in range(n)]
     for k in range(1, n):
         peer = (c + k) % n
@@ -372,13 +402,13 @@
                     ctx=peer,
                 )
             )
-    gather_forward(z1, z1_ids)
+    gather_forward(pieces(z1), z1_ids)
     for copy in loads[1:]:
         copy.wait()
-    gather_end(z1, z1_ids)
+    gather_end(pieces(z1), z1_ids)
     u1[...] = dot(k1[...], flat(z1), 1, 0)
-    v1[...] = gelu_of(u1[...]).astype(bf16)
-    mixed1 = mixed(p1, v1)
+    v_all[c] = gelu_of(u1[...]).astype(bf16)
+    mixed1 = mixed(p1, v_all.at[c])
     rs_ids = scatter_start(0, mixed1)
     for copy in own_grad:
         copy.wait()
@@ -391,17 +421,19 @@
                 grad_ids[k][h],
                 ctx=origin,
             ).wait_recv()
-    g2_ids = gather_start(g2)
+    g2_ids = gather_start(pieces(g2))
+    v_ids = push_start(lambda peer: v_all.at[c], lambda at: v_all.at[at])
+    z_ids = push_start(lambda peer: z1.at[peer, quarter(m), :], lambda at: z_rows.at[at, quarter(m), :])
     scatter_cross(0, rs_ids, mixed1)
-    gather_forward(g2, g2_ids)
+    gather_forward(pieces(g2), g2_ids)
     middle = x_v[...].astype(f32) + scatter_end(0, rs_ids, mixed1)
     mid_v[...] = middle.astype(bf16)
     z2[m] = gelu_of(mid_v[...].astype(f32)).astype(bf16)
-    z2_ids = gather_start(z2)
-    gather_end(g2, g2_ids)
+    z2_ids = gather_start(pieces(z2))
+    gather_end(pieces(g2), g2_ids)
     gh[...] = dot(p2[...], flat(g2), 1, 0)
-    gather_forward(z2, z2_ids)
-    gather_end(z2, z2_ids)
+    gather_forward(pieces(z2), z2_ids)
+    gather_end(pieces(z2), z2_ids)
     u2[...] = dot(k2[...], flat(z2), 1, 0)
     v2[...] = gelu_of(u2[...]).astype(bf16)
     gu2[...] = (gh[...] * slope_of(u2[...])).astype(bf16)
@@ -416,36 +448,46 @@
     out_ids = scatter_start(2, mixed2)
     previous = g2[m].astype(f32) + scatter_end(1, rs_ids, spread2) * mid_slope
     g1[m] = previous.astype(bf16)
-    g1_ids = gather_start(g1)
+    g1_ids = gather_start(pieces(g1))
     line_relay(0, 1)
-    gather_forward(g1, g1_ids)
-    gather_end(g1, g1_ids)
+    gather_forward(pieces(g1), g1_ids)
+    gather_end(pieces(g1), g1_ids)
+    g_ids = push_start(lambda peer: g1.at[peer, quarter(m), :], lambda at: g_rows.at[at, quarter(m), :])
     gh[...] = dot(p1[...], flat(g1), 1, 0)
-    gu1[...] = (gh[...] * slope_of(u1[...])).astype(bf16)
-    spread1 = spread(k1, gu1)
+    gu_all[c] = (gh[...] * slope_of(u1[...])).astype(bf16)
+    gu_ids = push_start(lambda peer: gu_all.at[c], lambda at: gu_all.at[at])
+    spread1 = spread(k1, gu_all.at[c])
     rs_ids = scatter_start(3, spread1)
-    products(2, gu1, z1)
-    products(3, v1, g1)
-    line_first(2, 3)
     line_relay(1, 1)
+    scatter_cross(3, rs_ids, spread1)
+    push_wait(lambda at: z_rows.at[at, quarter(m), :], z_ids)
+    z_row_ids = gather_start(row_views(z_rows))
+    scatter_cross(2, out_ids, mixed2)
     for i in (0, 1):
         for hop in range(2, n - 1):
             line_relay(i, hop)
-    scatter_cross(3, rs_ids, spread1)
-    scatter_cross(2, out_ids, mixed2)
     first_slope = slope_of(x_v[...].astype(f32))
     previous = g1[m].astype(f32) + scatter_end(3, rs_ids, spread1) * first_slope
     gx_o[...] = previous.astype(bf16)
+    gather_forward(row_views(z_rows), z_row_ids)
+    push_wait(lambda at: g_rows.at[at, quarter(m), :], g_ids)
+    g_row_ids = gather_start(row_views(g_rows))
     result = mid_v[...].astype(f32) + scatter_end(2, out_ids, mixed2)
     out_o[...] = result.astype(bf16)
-    for hop in range(1, n - 1):
-        for i in (2, 3):
-            line_relay(i, hop)
-    for i, result_o in enumerate((gp2_o, gk2_o, gk1_o, gp1_o)):
+    gather_end(row_views(z_rows), z_row_ids)
+    z_rows[c] = z1[c]
+    g_rows[c] = g1[c]
+    gather_forward(row_views(g_rows), g_row_ids)
+    push_wait(lambda at: gu_all.at[at], gu_ids)
+    gk1_o[...] = sum(dot(gu_all[k], z_rows[k], 1, 1) for k in range(n))
+    push_wait(lambda at: v_all.at[at], v_ids)
+    gather_end(row_views(g_rows), g_row_ids)
+    gp1_o[...] = sum(dot(v_all[k], g_rows[k], 1, 1) for k in range(n))
+    for i, result_o in enumerate((gp2_o, gk2_o)):
         line_end(i, result_o)
     for copy in sent:
         copy.wait_send()
-    for i in range(4):
+    for i in range(2):
         line_drain(i)
 
 
@@ -463,9 +505,9 @@
     width = k1.shape[1]
     bf16, f32 = jnp.bfloat16, jnp.float32
     full = pltpu.VMEM((parts, rows, bins), bf16)
-    shares = pltpu.VMEM((4, n, width, rows), bf16)
-    copies = 24 + 8 * n + grad.shape[0] * n
-    inner = [pltpu.VMEM((width, bins), f32)] * 2 + [pltpu.VMEM((width, bins), bf16)] * 4
+    shares = pltpu.VMEM((2, n, width, rows), bf16)
+    copies = 24 + 4 * n + 4 * n + 6 * (n - 1) + grad.shape[0] * n
+    inner = [pltpu.VMEM((width, bins), f32)] * 3 + [pltpu.VMEM((width, bins), bf16)] * 2
     results = pl.pallas_call(
         functools.partial(whole_kernel, n),
         out_shape=[
@@ -486,7 +528,10 @@
         ]
         + inner
         + [
-            pltpu.VMEM((width, bins), f32),
+            pltpu.VMEM((n, width, bins), bf16),
+            pltpu.VMEM((n, width, bins), bf16),
+            pltpu.VMEM((n, rows, bins), bf16),
+            pltpu.VMEM((n, rows, bins), bf16),
             pltpu.VMEM((4, 3, rows, bins), bf16),
             pltpu.VMEM((4, 3, rows, bins), bf16),
             shares, shares, shares,

time: 85.4 us -> 76.6 us (0.90)
  Pallas kernels: 84.6 us -> 75.1 us
    pallas_call x1, Pallas kernels: 81.6 us -> 72 us  [short_sequence(): pl.pallas_call(functools.partial(whole_kernel, n), out_shape=[jax.ShapeDt...]
where the time goes in v3:
time: 76.6 us; the launch traced here: 75.7 us
  Pallas kernels  75.1 us (98%)
    pallas_call x1, Pallas kernels, short_sequence(): pl.pallas_call(functools.partial(whole_kernel, n), out_shape=[jax.ShapeDt...  72 us
    pallas_call x1, Pallas kernels, short_sequence(): pl.pallas_call(write_results, out_shape=[jax.ShapeDtypeStruct((rows, bins...  3.05 us

profile of v3, /device:TPU:0, one launch (start us, length us, event | category | flops | bytes accessed | tf_op | source)
XLA Modules:
  0.0 75.7 jit_solution(3795802419291813660)
XLA Ops:
  0.6 72.0 %blocks.1 = (bf16[384,256]{1,0:T(8,128)(2,1)}, bf16[384,256]{1,0:T(8,128)(2,1)}, f32[192,384]{1,0:T(8,128)}, f32[192,384]{1,0:T(8,128)}, f32[192,384]{1,0:T(8,128)}, /*index=5*/f32[192,384]{1,0:T(8,128)}) custom-call(bf16[384,256]{1,0:T(8,128)(2,1)} %x_h.1, bf16[3,192,1536]{2,1,0:T(8,128)(2,1)} %k1_h.1, bf16[192,1536]{1,0:T(8,128)(2,1)} %bitcast.4, ...), custom_call_target="tpu_custom_call" | custom-call | tf_op jit(solution)/shard_map/blocks/pallas_call | solution.py:511
  72.7 3.0 %results.1 = (bf16[384,256]{1,0:T(8,128)(2,1)}, bf16[384,256]{1,0:T(8,128)(2,1)}, f32[3,192,384]{2,1,0:T(8,128)}, f32[192,384]{1,0:T(8,128)}, f32[3,192,384]{2,1,0:T(8,128)}, /*index=5*/f32[192,384]{1,0:T(8,128)}) custom-call(bf16[384,256]{1,0:T(8,128)(2,1)} %get-tuple-element.18.out_i, bf16[384,256]{1,0:T(8,128)(2,1)} %get-tuple-element.19.gx_i, ...), custom_call_target="tpu_custom_call" | custom-call | tf_op jit(solution)/shard_map/results/pallas_call | solution.py:549

commit v4 on v3

--- a/solution.py
+++ b/solution.py
@@ -189,11 +189,11 @@
     counter = iter(range(send.shape[0]))
     sent = []
 
-    def remote(src, dst, i, **device):
+    def remote(src, dst, i, by=None, **device):
         return pltpu.make_async_remote_copy(
             src_ref=src,
             dst_ref=dst,
-            send_sem=send.at[i],
+            send_sem=send.at[i if by is None else by],
             recv_sem=recv.at[i],
             device_id=device,
             device_id_type=pl.DeviceIdType.MESH,
@@ -270,6 +270,64 @@
         for k in range(1, n):
             origin = (c + n - k) % n
             remote(target(origin), target(origin), ids[k], ctx=origin).wait_recv()
+
+    fan_ids = [next(counter) for _ in range(2 * n)]
+
+    def fan_copy(target, origin, k, by, peer):
+        return remote(target(origin), target(origin), fan_ids[k], by=fan_ids[by], ctx=peer)
+
+    def fan_own(target, act):
+        for k in range(1, n):
+            peer = (c + k) % n
+            relayed = ((peer == n - 1) & (c < n - 2)) | ((peer == 0) & (c > 1))
+
+            @pl.when(jnp.logical_not(relayed))
+            def _():
+                act(fan_copy(target, c, k, k, peer))
+
+    def fan_passed(target, act):
+        for origin in range(n - 2):
+
+            @pl.when(c == n - 2)
+            def _():
+                act(target, origin, n - 2 - origin, n - 1 - origin, n - 1)
+
+        for origin in range(n - 1, 1, -1):
+
+            @pl.when(c == 1)
+            def _():
+                act(target, origin, n + 1 - origin, n - origin, 0)
+
+    def pass_on(target, origin, arrived, k, peer):
+        fan_copy(target, origin, arrived, arrived, peer).wait_recv()
+        fan_copy(target, origin, k, n + origin, peer).start()
+
+    def pass_done(target, origin, arrived, k, peer):
+        fan_copy(target, origin, k, n + origin, peer).wait_send()
+
+    def fan_wait(target):
+        for k in range(1, n):
+            origin = (c + n - k) % n
+            waited = ((c == n - 2) & (origin < n - 2)) | ((c == 1) & (origin > 1))
+
+            @pl.when(jnp.logical_not(waited))
+            def _():
+                fan_copy(target, origin, k, k, origin).wait_recv()
+
+    def pair_start(buf):
+        ids = [next(counter) for _ in range(n)]
+        for k in range(1, n):
+            own = buf.at[(c + k) % n, half(m % 2), :]
+            start(remote(own, own, ids[k], mp=sib))
+        return ids
+
+    def pair_end(buf, ids):
+        for k in range(1, n):
+            other = buf.at[(c + k) % n, half(1 - m % 2), :]
+            remote(other, other, ids[k], mp=sib).wait_recv()
+
+    def half(b):
+        return pl.ds(pl.multiple_of(b * (rows // 2), 16), rows // 2)
 
     def quarter(b):
         return pl.ds(pl.multiple_of(b * (rows // 4), 16), rows // 4)
@@ -423,7 +481,9 @@
             ).wait_recv()
     g2_ids = gather_start(pieces(g2))
     v_ids = push_start(lambda peer: v_all.at[c], lambda at: v_all.at[at])
-    z_ids = push_start(lambda peer: z1.at[peer, quarter(m), :], lambda at: z_rows.at[at, quarter(m), :])
+    z_ids = push_start(
+        lambda peer: z1.at[peer, half(m % 2), :], lambda at: z_rows.at[at, half(m % 2), :]
+    )
     scatter_cross(0, rs_ids, mixed1)
     gather_forward(pieces(g2), g2_ids)
     middle = x_v[...].astype(f32) + scatter_end(0, rs_ids, mixed1)
@@ -449,36 +509,36 @@
     previous = g2[m].astype(f32) + scatter_end(1, rs_ids, spread2) * mid_slope
     g1[m] = previous.astype(bf16)
     g1_ids = gather_start(pieces(g1))
+    push_wait(lambda at: z_rows.at[at, half(m % 2), :], z_ids)
+    z_row_ids = pair_start(z_rows)
     line_relay(0, 1)
     gather_forward(pieces(g1), g1_ids)
     gather_end(pieces(g1), g1_ids)
     g_ids = push_start(lambda peer: g1.at[peer, quarter(m), :], lambda at: g_rows.at[at, quarter(m), :])
     gh[...] = dot(p1[...], flat(g1), 1, 0)
     gu_all[c] = (gh[...] * slope_of(u1[...])).astype(bf16)
-    gu_ids = push_start(lambda peer: gu_all.at[c], lambda at: gu_all.at[at])
+    fan_own(lambda at: gu_all.at[at], lambda copy: copy.start())
     spread1 = spread(k1, gu_all.at[c])
     rs_ids = scatter_start(3, spread1)
     line_relay(1, 1)
     scatter_cross(3, rs_ids, spread1)
-    push_wait(lambda at: z_rows.at[at, quarter(m), :], z_ids)
-    z_row_ids = gather_start(row_views(z_rows))
     scatter_cross(2, out_ids, mixed2)
     for i in (0, 1):
         for hop in range(2, n - 1):
             line_relay(i, hop)
+    push_wait(lambda at: g_rows.at[at, quarter(m), :], g_ids)
+    g_row_ids = gather_start(row_views(g_rows))
+    fan_passed(lambda at: gu_all.at[at], pass_on)
     first_slope = slope_of(x_v[...].astype(f32))
     previous = g1[m].astype(f32) + scatter_end(3, rs_ids, spread1) * first_slope
     gx_o[...] = previous.astype(bf16)
-    gather_forward(row_views(z_rows), z_row_ids)
-    push_wait(lambda at: g_rows.at[at, quarter(m), :], g_ids)
-    g_row_ids = gather_start(row_views(g_rows))
     result = mid_v[...].astype(f32) + scatter_end(2, out_ids, mixed2)
     out_o[...] = result.astype(bf16)
-    gather_end(row_views(z_rows), z_row_ids)
+    gather_forward(row_views(g_rows), g_row_ids)
+    pair_end(z_rows, z_row_ids)
     z_rows[c] = z1[c]
     g_rows[c] = g1[c]
-    gather_forward(row_views(g_rows), g_row_ids)
-    push_wait(lambda at: gu_all.at[at], gu_ids)
+    fan_wait(lambda at: gu_all.at[at])
     gk1_o[...] = sum(dot(gu_all[k], z_rows[k], 1, 1) for k in range(n))
     push_wait(lambda at: v_all.at[at], v_ids)
     gather_end(row_views(g_rows), g_row_ids)
@@ -487,16 +547,27 @@
         line_end(i, result_o)
     for copy in sent:
         copy.wait_send()
+    fan_own(lambda at: gu_all.at[at], lambda copy: copy.wait_send())
+    fan_passed(lambda at: gu_all.at[at], pass_done)
     for i in range(2):
         line_drain(i)
 
 
-def write_results(out_i, gx_i, gk1_i, gp1_i, gk2_i, gp2_i, out_o, gx_o, gk1_o, gp1_o, gk2_o, gp2_o):
-    for taken, given in ((out_i, out_o), (gx_i, gx_o), (gp1_i, gp1_o), (gp2_i, gp2_o)):
-        given[...] = taken[...]
-    for taken, given in ((gk1_i, gk1_o), (gk2_i, gk2_o)):
-        given[...] = jnp.zeros_like(given)
-        given[1] = taken[...]
+def write_results(
+    out_i, gx_i, gk1_i, gp1_i, gk2_i, gp2_i, out_o, gx_o, gk1_o, gp1_o, gk2_o, gp2_o, zero, sems
+):
+    plain = [(gp1_i, gp1_o), (gp2_i, gp2_o), (gk1_i, gk1_o.at[1]), (gk2_i, gk2_o.at[1])]
+    plain += [(out_i, out_o), (gx_i, gx_o)]
+    copies = [pltpu.make_async_copy(src, dst, sems.at[i]) for i, (src, dst) in enumerate(plain)]
+    for copy in copies:
+        copy.start()
+    zero[...] = jnp.zeros_like(zero)
+    empty = [gk1_o.at[0], gk1_o.at[2], gk2_o.at[0], gk2_o.at[2]]
+    fills = [pltpu.make_async_copy(zero, dst, sems.at[6 + i]) for i, dst in enumerate(empty)]
+    for copy in fills:
+        copy.start()
+    for copy in copies + fills:
+        copy.wait()
 
 
 def short_sequence(sizes, x, k1, p1, k2, p2, grad):
@@ -506,7 +577,7 @@
     bf16, f32 = jnp.bfloat16, jnp.float32
     full = pltpu.VMEM((parts, rows, bins), bf16)
     shares = pltpu.VMEM((2, n, width, rows), bf16)
-    copies = 24 + 4 * n + 4 * n + 6 * (n - 1) + grad.shape[0] * n
+    copies = 24 + 4 * n + 6 * n + 3 * (n - 1) + grad.shape[0] * n
     inner = [pltpu.VMEM((width, bins), f32)] * 3 + [pltpu.VMEM((width, bins), bf16)] * 2
     results = pl.pallas_call(
         functools.partial(whole_kernel, n),
@@ -554,7 +625,8 @@
             taps, points, taps, points,
         ],
         in_specs=[pl.BlockSpec(memory_space=pltpu.VMEM)] * 6,
-        out_specs=[pl.BlockSpec(memory_space=pltpu.VMEM)] * 6,
+        out_specs=[pl.BlockSpec(memory_space=pl.ANY)] * 6,
+        scratch_shapes=[pltpu.VMEM((width, rows), f32), pltpu.SemaphoreType.DMA((10,))],
         name="results",
     )(*results)
     return out, gx, gk1, gp1.T, gk2, gp2.T

time: 76.6 us -> 77.2 us (level)
  Pallas kernels: 75.1 us -> 76.4 us
    pallas_call x1, Pallas kernels: 72 us -> 73.4 us  [short_sequence(): pl.pallas_call(functools.partial(whole_kernel, n), out_shape=[jax.ShapeDt...]
where the time goes in v4:
time: 77.2 us; the launch traced here: 77 us
  Pallas kernels  76.4 us (99%)
    pallas_call x1, Pallas kernels, short_sequence(): pl.pallas_call(functools.partial(whole_kernel, n), out_shape=[jax.ShapeDt...  73.4 us
    pallas_call x1, Pallas kernels, short_sequence(): pl.pallas_call(write_results, out_shape=[jax.ShapeDtypeStruct((rows, bins...  3.04 us

profile of v4, /device:TPU:0, one launch (start us, length us, event | category | flops | bytes accessed | tf_op | source)
XLA Modules:
  0.0 77.0 jit_solution(1243106071963141407)
XLA Ops:
  0.6 73.4 %blocks.1 = (bf16[384,256]{1,0:T(8,128)(2,1)}, bf16[384,256]{1,0:T(8,128)(2,1)}, f32[192,384]{1,0:T(8,128)}, f32[192,384]{1,0:T(8,128)}, f32[192,384]{1,0:T(8,128)}, /*index=5*/f32[192,384]{1,0:T(8,128)}) custom-call(bf16[384,256]{1,0:T(8,128)(2,1)} %x_h.1, bf16[3,192,1536]{2,1,0:T(8,128)(2,1)} %k1_h.1, bf16[192,1536]{1,0:T(8,128)(2,1)} %bitcast.4, ...), custom_call_target="tpu_custom_call" | custom-call | tf_op jit(solution)/shard_map/blocks/pallas_call | solution.py:582
  74.0 3.0 %results.1 = (bf16[384,256]{1,0:T(8,128)(2,1)}, bf16[384,256]{1,0:T(8,128)(2,1)}, f32[3,192,384]{2,1,0:T(8,128)}, f32[192,384]{1,0:T(8,128)}, f32[3,192,384]{2,1,0:T(8,128)}, /*index=5*/f32[192,384]{1,0:T(8,128)}) custom-call(bf16[384,256]{1,0:T(8,128)(2,1)} %get-tuple-element.18.out_i, bf16[384,256]{1,0:T(8,128)(2,1)} %get-tuple-element.19.gx_i, ...), custom_call_target="tpu_custom_call" | custom-call | tf_op jit(solution)/shard_map/results/pallas_call | solution.py:620

commit v5 on v4

--- a/solution.py
+++ b/solution.py
@@ -509,10 +509,10 @@
     previous = g2[m].astype(f32) + scatter_end(1, rs_ids, spread2) * mid_slope
     g1[m] = previous.astype(bf16)
     g1_ids = gather_start(pieces(g1))
+    gather_forward(pieces(g1), g1_ids)
     push_wait(lambda at: z_rows.at[at, half(m % 2), :], z_ids)
     z_row_ids = pair_start(z_rows)
     line_relay(0, 1)
-    gather_forward(pieces(g1), g1_ids)
     gather_end(pieces(g1), g1_ids)
     g_ids = push_start(lambda peer: g1.at[peer, quarter(m), :], lambda at: g_rows.at[at, quarter(m), :])
     gh[...] = dot(p1[...], flat(g1), 1, 0)
@@ -624,7 +624,7 @@
             jax.ShapeDtypeStruct((rows, bins), bf16),
             taps, points, taps, points,
         ],
-        in_specs=[pl.BlockSpec(memory_space=pltpu.VMEM)] * 6,
+        in_specs=[pl.BlockSpec(memory_space=pl.ANY)] * 6,
         out_specs=[pl.BlockSpec(memory_space=pl.ANY)] * 6,
         scratch_shapes=[pltpu.VMEM((width, rows), f32), pltpu.SemaphoreType.DMA((10,))],
         name="results",

time: 77.2 us -> 125 us (1.62)
  Pallas kernels: 76.4 us -> 124 us
    pallas_call x1, Pallas kernels: 3.04 us -> 48.8 us  [short_sequence(): pl.pallas_call(write_results, out_shape=[jax.ShapeDtypeStruct((rows, bins...]
    pallas_call x1, Pallas kernels: 73.4 us -> 74.9 us  [short_sequence(): pl.pallas_call(functools.partial(whole_kernel, n), out_shape=[jax.ShapeDt...]
where the time goes in v5:
time: 125 us; the launch traced here: 124 us
  Pallas kernels  124 us (99%)
    pallas_call x1, Pallas kernels, short_sequence(): pl.pallas_call(functools.partial(whole_kernel, n), out_shape=[jax.ShapeDt...  74.9 us
    pallas_call x1, Pallas kernels, short_sequence(): pl.pallas_call(write_results, out_shape=[jax.ShapeDtypeStruct((rows, bins...  48.8 us

profile of v5, /device:TPU:0, one launch (start us, length us, event | category | flops | bytes accessed | tf_op | source)
XLA Modules:
  0.0 124.4 jit_solution(8586858899304302686)
XLA Ops:
  0.6 74.9 %blocks.1 = (bf16[384,256]{1,0:T(8,128)(2,1)}, bf16[384,256]{1,0:T(8,128)(2,1)}, f32[192,384]{1,0:T(8,128)}, f32[192,384]{1,0:T(8,128)}, f32[192,384]{1,0:T(8,128)}, /*index=5*/f32[192,384]{1,0:T(8,128)}) custom-call(bf16[384,256]{1,0:T(8,128)(2,1)} %x_h.1, bf16[3,192,1536]{2,1,0:T(8,128)(2,1)} %k1_h.1, bf16[192,1536]{1,0:T(8,128)(2,1)} %bitcast.4, ...), custom_call_target="tpu_custom_call" | custom-call | tf_op jit(solution)/shard_map/blocks/pallas_call | solution.py:582
  75.6 48.8 %results.1 = (bf16[384,256]{1,0:T(8,128)(2,1)}, bf16[384,256]{1,0:T(8,128)(2,1)}, f32[3,192,384]{2,1,0:T(8,128)}, f32[192,384]{1,0:T(8,128)}, f32[3,192,384]{2,1,0:T(8,128)}, /*index=5*/f32[192,384]{1,0:T(8,128)}) custom-call(bf16[384,256]{1,0:T(8,128)(2,1)} %get-tuple-element.18.out_i, bf16[384,256]{1,0:T(8,128)(2,1)} %get-tuple-element.19.gx_i, ...), custom_call_target="tpu_custom_call" | custom-call | tf_op jit(solution)/shard_map/results/pallas_call | solution.py:620
